TPU v7x, 1024 devices: a whole 4x8x16 slice. The times are simulated.
1024 devices in a mesh: group: 64 (over x, z), row: 16 (over y, core).
Axes of the slice: x: 4, y: 8, z: 16, core: 2. Of those that a mesh axis runs over, the one named last changes fastest.
Arguments:
- pooled_grad: bfloat16 [4096, 64, 128], P(('row', 'group')), may hold values from -0.59765625 to 0.59765625
- bag_ids: int32 [64, 40, 4096], P('group'), may hold values from 0 to 32767
- bag_len: int32 [64, 4096], P('group'), may hold values from 1 to 40
- table_rows: float32 [64, 32768, 128], P('group', 'row'), may hold values from -3 to 3
- row_state: float32 [64, 32768], P('group', 'row'), may hold values from 0.05 to 2
Outputs:
- new_rows: float32 [64, 32768, 128], P('group', 'row')
- new_state: float32 [64, 32768], P('group', 'row')
All inputs are finite; a program needn't handle non-finite values.
Results may differ from a plain program's by a relative error of at most 0.0003.
Values may be sent and summed in bfloat16 or wider, within the bound.
A program may use at most 32 MiB of HBM per device.

v0:
```python
import jax
import jax.numpy as jnp
from jax import lax
from jax.sharding import PartitionSpec as P


def accumulate(running, pooled_rows, first_row, bag_ids, bag_len, row_base):
    count_rows = pooled_rows.shape[0]
    block = 256
    touched = running.shape[1]
    slot_count = bag_ids.shape[1]

    def advance(turn, carried):
        offset = first_row + turn * block
        part_rows = lax.dynamic_slice_in_dim(pooled_rows, turn * block, block, 0)
        id_block = lax.dynamic_slice_in_dim(bag_ids, offset, block, 2)
        len_block = lax.dynamic_slice_in_dim(bag_len, offset, block, 1)
        columns = lax.broadcasted_iota(jnp.int32, (1, 1, touched), 2)
        counts_tile = jnp.zeros((id_block.shape[0], block, touched), jnp.bfloat16)
        for slot in range(slot_count):
            local_ids = jnp.where(slot < len_block, id_block[:, slot, :] - row_base, -1)
            counts_tile = counts_tile + (local_ids[:, :, None] == columns).astype(jnp.bfloat16)
        return carried + jnp.einsum(
            "tbu,bte->tue", counts_tile, part_rows, preferred_element_type=jnp.float32
        )

    return lax.fori_loop(0, count_rows // block, advance, running)


def on_device(pooled_grad, bag_ids, bag_len, table_rows, row_state):
    owned = lax.all_to_all(pooled_grad, "group", split_axis=1, concat_axis=0, tiled=True)
    touched = row_state.shape[1]
    row_base = lax.axis_index("row") * touched
    empty = jnp.zeros(table_rows.shape, jnp.float32)
    everything = lax.all_gather(owned, "row", axis=0, tiled=True)
    row_grad = accumulate(empty, everything, 0, bag_ids, bag_len, row_base)
    new_state = row_state + jnp.mean(row_grad * row_grad, axis=2)
    new_rows = table_rows - 0.5 * row_grad / (jnp.sqrt(new_state)[:, :, None] + 1e-08)
    return (new_rows, new_state)


def solution(mesh):
    placed = (
        P(("row", "group"), None, None),
        P("group", None, None),
        P("group", None),
        P("group", "row", None),
        P("group", "row"),
    )
    return jax.shard_map(
        on_device,
        mesh=mesh,
        in_specs=placed,
        out_specs=(P("group", "row", None), P("group", "row")),
        check_vma=False,
    )
```

profile of v0, /device:TPU:1, one launch (start us, length us, event | category | flops | bytes accessed | tf_op | source)
XLA Modules:
  0.0 350.0 jit_solution(884093243993780989)
XLA Ops:
  8.1 36.2 %all_to_all.18 = bf16[4,64,128]{2,0,1:T(4,128)(2,1)} all-to-all(bf16[4,64,128]{2,0,1:T(4,128)(2,1)S(1)} %copy.9), channel_id=1, replica_groups=mesh['group'=64,'row'=16] {'group'}, dimensions={1} | all-to-all | bytes 131072 | tf_op jit(solution)/shard_map/all_to_all | solution.py:31
  44.4 38.2 %all-gather.2.cloned.1.call-done = bf16[4096,1,128]{2,0,1:T(8,128)(2,1)} async-done(((bf16[256,1,128]{2,0,1:T(8,128)(2,1)}), bf16[4096,1,128]{2,0,1:T(8,128)(2,1)}) %all-gather.2.cloned.1.call-update) | async-done | bytes 1048592 | tf_op jit(solution)/shard_map/all_gather | solution.py:35
  82.5 258.0 %while.14 = (s32[]{:T(128)}, f32[1,2048,128]{2,1,0:T(8,128)S(1)}, s32[1,4096]{1,0:T(1,128)}, s32[1,40,4096]{2,1,0:T(8,128)}, s32[]{:T(128)}, /*index=5*/bf16[409...) while((s32[]{:T(128)}, f32[1,2048,128]{2,1,0:T(8,128)S(1)}, ...), condition=%wide.region_1.2_spmd.clone, body=%wide.region_0.1_spmd.clone.sunk | while | flops 218658864 | bytes 2291825 | solution.py:27
  83.2 1.0 compare_select_fusion.45
  84.3 1.2 compare_select_fusion.47
  85.4 1.1 compare_select_fusion.46
  86.6 12.0 %fusion.249 = f32[1,2048,128]{2,1,0:T(8,128)S(1)} fusion(f32[1,2048,128]{2,1,0:T(8,128)S(1)} %get-tuple-element.357, s32[256]{0:T(256)S(1)} %bitcast.323, s32[256]{0:T(256)S(1)} %bitcast.340, s32[256]{0:T(256)S(1)} %bitcast.341, s32[256]{0:T(256)S(1)} %bitcast.342, s32[256]{0:T(256)S(1)} %bitcast.343, s32[256]{0:T(256)S(1)} %bitcast.344, ...), kind=kOutput, calls=%fused_computation.1.clone.1 | convolution fusion | flops 218628096 | bytes 2203653 | tf_op jit(solution)/shard_map/while/body/eval_jaxpr/tbu,bte->tue/dot_general | solution.py:23
  99.3 1.1 compare_select_fusion.45
  100.3 1.2 compare_select_fusion.47
  101.5 1.1 compare_select_fusion.46
  102.6 12.0 %fusion.249 = f32[1,2048,128]{2,1,0:T(8,128)S(1)} fusion(f32[1,2048,128]{2,1,0:T(8,128)S(1)} %get-tuple-element.357, s32[256]{0:T(256)S(1)} %bitcast.323, s32[256]{0:T(256)S(1)} %bitcast.340, s32[256]{0:T(256)S(1)} %bitcast.341, s32[256]{0:T(256)S(1)} %bitcast.342, s32[256]{0:T(256)S(1)} %bitcast.343, s32[256]{0:T(256)S(1)} %bitcast.344, ...), kind=kOutput, calls=%fused_computation.1.clone.1 | convolution fusion | flops 218628096 | bytes 2203653 | tf_op jit(solution)/shard_map/while/body/eval_jaxpr/tbu,bte->tue/dot_general | solution.py:23
  115.3 1.0 compare_select_fusion.45
  116.3 1.2 compare_select_fusion.47
  117.5 1.1 compare_select_fusion.46
  118.6 12.0 %fusion.249 = f32[1,2048,128]{2,1,0:T(8,128)S(1)} fusion(f32[1,2048,128]{2,1,0:T(8,128)S(1)} %get-tuple-element.357, s32[256]{0:T(256)S(1)} %bitcast.323, s32[256]{0:T(256)S(1)} %bitcast.340, s32[256]{0:T(256)S(1)} %bitcast.341, s32[256]{0:T(256)S(1)} %bitcast.342, s32[256]{0:T(256)S(1)} %bitcast.343, s32[256]{0:T(256)S(1)} %bitcast.344, ...), kind=kOutput, calls=%fused_computation.1.clone.1 | convolution fusion | flops 218628096 | bytes 2203653 | tf_op jit(solution)/shard_map/while/body/eval_jaxpr/tbu,bte->tue/dot_general | solution.py:23
  131.3 1.0 compare_select_fusion.45
  132.3 1.2 compare_select_fusion.47
  133.5 1.1 compare_select_fusion.46
  134.6 12.0 %fusion.249 = f32[1,2048,128]{2,1,0:T(8,128)S(1)} fusion(f32[1,2048,128]{2,1,0:T(8,128)S(1)} %get-tuple-element.357, s32[256]{0:T(256)S(1)} %bitcast.323, s32[256]{0:T(256)S(1)} %bitcast.340, s32[256]{0:T(256)S(1)} %bitcast.341, s32[256]{0:T(256)S(1)} %bitcast.342, s32[256]{0:T(256)S(1)} %bitcast.343, s32[256]{0:T(256)S(1)} %bitcast.344, ...), kind=kOutput, calls=%fused_computation.1.clone.1 | convolution fusion | flops 218628096 | bytes 2203653 | tf_op jit(solution)/shard_map/while/body/eval_jaxpr/tbu,bte->tue/dot_general | solution.py:23
  148.3 1.3 compare_select_fusion.47
  149.6 1.3 compare_select_fusion.46
  150.9 12.0 %fusion.249 = f32[1,2048,128]{2,1,0:T(8,128)S(1)} fusion(f32[1,2048,128]{2,1,0:T(8,128)S(1)} %get-tuple-element.357, s32[256]{0:T(256)S(1)} %bitcast.323, s32[256]{0:T(256)S(1)} %bitcast.340, s32[256]{0:T(256)S(1)} %bitcast.341, s32[256]{0:T(256)S(1)} %bitcast.342, s32[256]{0:T(256)S(1)} %bitcast.343, s32[256]{0:T(256)S(1)} %bitcast.344, ...), kind=kOutput, calls=%fused_computation.1.clone.1 | convolution fusion | flops 218628096 | bytes 2203653 | tf_op jit(solution)/shard_map/while/body/eval_jaxpr/tbu,bte->tue/dot_general | solution.py:23
  163.6 1.0 compare_select_fusion.45
  164.6 1.2 compare_select_fusion.47
  165.7 1.3 compare_select_fusion.46
  167.0 11.9 %fusion.249 = f32[1,2048,128]{2,1,0:T(8,128)S(1)} fusion(f32[1,2048,128]{2,1,0:T(8,128)S(1)} %get-tuple-element.357, s32[256]{0:T(256)S(1)} %bitcast.323, s32[256]{0:T(256)S(1)} %bitcast.340, s32[256]{0:T(256)S(1)} %bitcast.341, s32[256]{0:T(256)S(1)} %bitcast.342, s32[256]{0:T(256)S(1)} %bitcast.343, s32[256]{0:T(256)S(1)} %bitcast.344, ...), kind=kOutput, calls=%fused_computation.1.clone.1 | convolution fusion | flops 218628096 | bytes 2203653 | tf_op jit(solution)/shard_map/while/body/eval_jaxpr/tbu,bte->tue/dot_general | solution.py:23
  179.7 1.0 compare_select_fusion.45
  180.7 1.2 compare_select_fusion.47
  181.8 1.3 compare_select_fusion.46
  183.2 12.0 %fusion.249 = f32[1,2048,128]{2,1,0:T(8,128)S(1)} fusion(f32[1,2048,128]{2,1,0:T(8,128)S(1)} %get-tuple-element.357, s32[256]{0:T(256)S(1)} %bitcast.323, s32[256]{0:T(256)S(1)} %bitcast.340, s32[256]{0:T(256)S(1)} %bitcast.341, s32[256]{0:T(256)S(1)} %bitcast.342, s32[256]{0:T(256)S(1)} %bitcast.343, s32[256]{0:T(256)S(1)} %bitcast.344, ...), kind=kOutput, calls=%fused_computation.1.clone.1 | convolution fusion | flops 218628096 | bytes 2203653 | tf_op jit(solution)/shard_map/while/body/eval_jaxpr/tbu,bte->tue/dot_general | solution.py:23
  195.9 1.0 compare_select_fusion.45
  196.8 1.2 compare_select_fusion.47
  198.1 1.3 compare_select_fusion.46
  199.4 12.0 %fusion.249 = f32[1,2048,128]{2,1,0:T(8,128)S(1)} fusion(f32[1,2048,128]{2,1,0:T(8,128)S(1)} %get-tuple-element.357, s32[256]{0:T(256)S(1)} %bitcast.323, s32[256]{0:T(256)S(1)} %bitcast.340, s32[256]{0:T(256)S(1)} %bitcast.341, s32[256]{0:T(256)S(1)} %bitcast.342, s32[256]{0:T(256)S(1)} %bitcast.343, s32[256]{0:T(256)S(1)} %bitcast.344, ...), kind=kOutput, calls=%fused_computation.1.clone.1 | convolution fusion | flops 218628096 | bytes 2203653 | tf_op jit(solution)/shard_map/while/body/eval_jaxpr/tbu,bte->tue/dot_general | solution.py:23
  213.0 1.3 compare_select_fusion.47
  214.3 1.1 compare_select_fusion.46
  215.5 12.0 %fusion.249 = f32[1,2048,128]{2,1,0:T(8,128)S(1)} fusion(f32[1,2048,128]{2,1,0:T(8,128)S(1)} %get-tuple-element.357, s32[256]{0:T(256)S(1)} %bitcast.323, s32[256]{0:T(256)S(1)} %bitcast.340, s32[256]{0:T(256)S(1)} %bitcast.341, s32[256]{0:T(256)S(1)} %bitcast.342, s32[256]{0:T(256)S(1)} %bitcast.343, s32[256]{0:T(256)S(1)} %bitcast.344, ...), kind=kOutput, calls=%fused_computation.1.clone.1 | convolution fusion | flops 218628096 | bytes 2203653 | tf_op jit(solution)/shard_map/while/body/eval_jaxpr/tbu,bte->tue/dot_general | solution.py:23
  228.1 1.0 compare_select_fusion.45
  229.1 1.3 compare_select_fusion.47
  230.4 1.1 compare_select_fusion.46
  231.6 12.0 %fusion.249 = f32[1,2048,128]{2,1,0:T(8,128)S(1)} fusion(f32[1,2048,128]{2,1,0:T(8,128)S(1)} %get-tuple-element.357, s32[256]{0:T(256)S(1)} %bitcast.323, s32[256]{0:T(256)S(1)} %bitcast.340, s32[256]{0:T(256)S(1)} %bitcast.341, s32[256]{0:T(256)S(1)} %bitcast.342, s32[256]{0:T(256)S(1)} %bitcast.343, s32[256]{0:T(256)S(1)} %bitcast.344, ...), kind=kOutput, calls=%fused_computation.1.clone.1 | convolution fusion | flops 218628096 | bytes 2203653 | tf_op jit(solution)/shard_map/while/body/eval_jaxpr/tbu,bte->tue/dot_general | solution.py:23
  244.3 1.0 compare_select_fusion.45
  245.2 1.2 compare_select_fusion.47
  246.5 1.4 compare_select_fusion.46
  247.8 12.0 %fusion.249 = f32[1,2048,128]{2,1,0:T(8,128)S(1)} fusion(f32[1,2048,128]{2,1,0:T(8,128)S(1)} %get-tuple-element.357, s32[256]{0:T(256)S(1)} %bitcast.323, s32[256]{0:T(256)S(1)} %bitcast.340, s32[256]{0:T(256)S(1)} %bitcast.341, s32[256]{0:T(256)S(1)} %bitcast.342, s32[256]{0:T(256)S(1)} %bitcast.343, s32[256]{0:T(256)S(1)} %bitcast.344, ...), kind=kOutput, calls=%fused_computation.1.clone.1 | convolution fusion | flops 218628096 | bytes 2203653 | tf_op jit(solution)/shard_map/while/body/eval_jaxpr/tbu,bte->tue/dot_general | solution.py:23
  261.5 1.2 compare_select_fusion.47
  262.7 1.1 compare_select_fusion.46
  263.8 12.0 %fusion.249 = f32[1,2048,128]{2,1,0:T(8,128)S(1)} fusion(f32[1,2048,128]{2,1,0:T(8,128)S(1)} %get-tuple-element.357, s32[256]{0:T(256)S(1)} %bitcast.323, s32[256]{0:T(256)S(1)} %bitcast.340, s32[256]{0:T(256)S(1)} %bitcast.341, s32[256]{0:T(256)S(1)} %bitcast.342, s32[256]{0:T(256)S(1)} %bitcast.343, s32[256]{0:T(256)S(1)} %bitcast.344, ...), kind=kOutput, calls=%fused_computation.1.clone.1 | convolution fusion | flops 218628096 | bytes 2203653 | tf_op jit(solution)/shard_map/while/body/eval_jaxpr/tbu,bte->tue/dot_general | solution.py:23
  276.5 1.0 compare_select_fusion.45
  277.5 1.4 compare_select_fusion.47
  278.9 1.3 compare_select_fusion.46
  280.1 12.0 %fusion.249 = f32[1,2048,128]{2,1,0:T(8,128)S(1)} fusion(f32[1,2048,128]{2,1,0:T(8,128)S(1)} %get-tuple-element.357, s32[256]{0:T(256)S(1)} %bitcast.323, s32[256]{0:T(256)S(1)} %bitcast.340, s32[256]{0:T(256)S(1)} %bitcast.341, s32[256]{0:T(256)S(1)} %bitcast.342, s32[256]{0:T(256)S(1)} %bitcast.343, s32[256]{0:T(256)S(1)} %bitcast.344, ...), kind=kOutput, calls=%fused_computation.1.clone.1 | convolution fusion | flops 218628096 | bytes 2203653 | tf_op jit(solution)/shard_map/while/body/eval_jaxpr/tbu,bte->tue/dot_general | solution.py:23
  293.8 1.2 compare_select_fusion.47
  295.0 1.3 compare_select_fusion.46
  296.3 12.0 %fusion.249 = f32[1,2048,128]{2,1,0:T(8,128)S(1)} fusion(f32[1,2048,128]{2,1,0:T(8,128)S(1)} %get-tuple-element.357, s32[256]{0:T(256)S(1)} %bitcast.323, s32[256]{0:T(256)S(1)} %bitcast.340, s32[256]{0:T(256)S(1)} %bitcast.341, s32[256]{0:T(256)S(1)} %bitcast.342, s32[256]{0:T(256)S(1)} %bitcast.343, s32[256]{0:T(256)S(1)} %bitcast.344, ...), kind=kOutput, calls=%fused_computation.1.clone.1 | convolution fusion | flops 218628096 | bytes 2203653 | tf_op jit(solution)/shard_map/while/body/eval_jaxpr/tbu,bte->tue/dot_general | solution.py:23
  308.9 1.0 compare_select_fusion.45
  309.9 1.2 compare_select_fusion.47
  311.1 1.3 compare_select_fusion.46
  312.4 12.0 %fusion.249 = f32[1,2048,128]{2,1,0:T(8,128)S(1)} fusion(f32[1,2048,128]{2,1,0:T(8,128)S(1)} %get-tuple-element.357, s32[256]{0:T(256)S(1)} %bitcast.323, s32[256]{0:T(256)S(1)} %bitcast.340, s32[256]{0:T(256)S(1)} %bitcast.341, s32[256]{0:T(256)S(1)} %bitcast.342, s32[256]{0:T(256)S(1)} %bitcast.343, s32[256]{0:T(256)S(1)} %bitcast.344, ...), kind=kOutput, calls=%fused_computation.1.clone.1 | convolution fusion | flops 218628096 | bytes 2203653 | tf_op jit(solution)/shard_map/while/body/eval_jaxpr/tbu,bte->tue/dot_general | solution.py:23
  325.1 1.0 compare_select_fusion.45
  326.1 1.2 compare_select_fusion.47
  327.3 1.3 compare_select_fusion.46
  328.6 12.0 %fusion.249 = f32[1,2048,128]{2,1,0:T(8,128)S(1)} fusion(f32[1,2048,128]{2,1,0:T(8,128)S(1)} %get-tuple-element.357, s32[256]{0:T(256)S(1)} %bitcast.323, s32[256]{0:T(256)S(1)} %bitcast.340, s32[256]{0:T(256)S(1)} %bitcast.341, s32[256]{0:T(256)S(1)} %bitcast.342, s32[256]{0:T(256)S(1)} %bitcast.343, s32[256]{0:T(256)S(1)} %bitcast.344, ...), kind=kOutput, calls=%fused_computation.1.clone.1 | convolution fusion | flops 218628096 | bytes 2203653 | tf_op jit(solution)/shard_map/while/body/eval_jaxpr/tbu,bte->tue/dot_general | solution.py:23
  341.9 1.3 divide_subtract_fusion
  (31 shorter events, 17.5 us)
Async XLA Ops:
  7.2 75.4 %all-gather.2.cloned.1.call-start = ((), (), s32[]{:S(2)}) async-start(), calls=%async_computation.1 | async-start | bytes 1114112 | tf_op jit(solution)/shard_map/all_gather | solution.py:35
  340.5 0.7 copy-start.1
  340.6 1.3 copy-start
Sparse Core Ops, SparseCore 0:
  44.5 38.0 all-gather.1
where the time goes:
time: 354 us; the launch traced here: 350 us
  matrix products  191 us (54%)
  other arithmetic  68.2 us (19%)
  waiting for transfers between devices  38.2 us (11%)
  blocking collectives  36.2 us (10%)
  between operations  14.1 us (4%)
    dot_general x16, matrix products, advance(): jnp.einsum('tbu,bte->tue', counts_tile, part_rows, preferred_element_type...  191 us
    select_n x64, other arithmetic, advance(): local_ids = jnp.where(slot < len_block, id_block[:, slot, :] - row_base, -1)  65.9 us
    all_gather x1, waiting for transfers between devices, on_device(): everything = lax.all_gather(owned, 'row', axis=0, tiled=True)  38.2 us
    all_to_all x1, blocking collectives, on_device(): lax.all_to_all(pooled_grad, 'group', split_axis=1, concat_axis=0, tiled=T...  36.2 us
  transfers between devices with their start and end apart: 1, of which 1 were waited for; matrix products, arithmetic and copies ran while one was open for 0% of the time, Pallas kernels for 0%

commit v1 on v0

v1 whole, which is shorter than its diff:
```python
import functools

import jax
import jax.numpy as jnp
from jax import lax
from jax.experimental import pallas as pl
from jax.experimental.pallas import tpu as pltpu
from jax.sharding import PartitionSpec as P

E = 128
SLOTS = 40
SAMPLES = 4096
GROUPS = 64
SHARDS = 16
WIDTH = 4
DEPTH = 16
RINGS = 8
EARLY = 6
VMEM = 60 * 2**20
TOUCHED = 2048
BLOCKS = 4
BLOCK = TOUCHED // BLOCKS
PARTS = 4
PART = TOUCHED // PARTS
FIELDS = 8
WORDS = TOUCHED // FIELDS
KEPT = 15
CHUNK = SAMPLES // SHARDS
MESH = pl.DeviceIdType.MESH


def prepare(ids, lens, keys, base):
    slot = lax.broadcasted_iota(jnp.int32, (8, 128), 0)

    def block(t, carry):
        lanes = pl.ds(pl.multiple_of(t * 128, 128), 128)
        used = lens[:, lanes]
        for q in range(SLOTS // 8):
            row = ids[pl.ds(8 * q, 8), lanes] - base
            key = ((row & (WORDS - 1)) * FIELDS) | (row >> 8)
            fits = ((row >> 11) == 0) & (slot + 8 * q < used)
            keys[q, pl.ds(pl.multiple_of(t * 8, 8), 8), :] = jnp.where(fits, key, -1)
        return carry

    lax.fori_loop(0, SAMPLES // 128, block, 0)


def compact(keys, words, adds, spill):
    spill[...] = jnp.full((8, 128), -1, jnp.int32)

    def block(b, carry):
        kept = [jnp.full((8, 128), -1, jnp.int32)] * KEPT
        lost = spill[...]
        for k in range(SLOTS):
            new = keys[k // 8, pl.ds(b * 64 + k % 8, 8, stride=8), :]
            for j in range(min(k + 1, KEPT)):
                kept[j], new = jnp.maximum(kept[j], new), jnp.minimum(kept[j], new)
            if k >= KEPT:
                lost = jnp.maximum(lost, new)
        spill[...] = lost
        word = [key >> 3 for key in kept]
        add = [jnp.where(key < 0, 0, jnp.left_shift(jnp.int32(1), (key & 7) * 4)) for key in kept]
        for j in range(KEPT - 1):
            same = word[j] == word[j + 1]
            add[j + 1] = add[j + 1] + jnp.where(same, add[j], 0)
            word[j] = jnp.where(same, -1, word[j])
        place = pl.ds(pl.multiple_of(b * 8, 8), 8)
        for j in range(KEPT):
            words[j, place, :] = word[j]
            adds[j, place, :] = add[j]
        return carry

    lax.fori_loop(0, SAMPLES // 1024, block, 0)


def count(words, adds, counts, slot):
    rows = lax.broadcasted_iota(jnp.int32, (16, 128), 0)
    for half in range(2):
        t = slot * 2 + half
        word = [jnp.broadcast_to(words[j, pl.ds(t, 1), :], (16, 128)) for j in range(KEPT)]
        add = [jnp.broadcast_to(adds[j, pl.ds(t, 1), :], (16, 128)) for j in range(KEPT)]

        def block(i, carry):
            here = rows + i * 16
            total = jnp.zeros((16, 128), jnp.int32)
            for j in range(KEPT):
                total = jnp.where(word[j] == here, add[j], total)
            for f in range(FIELDS):
                if f < FIELDS - 1:
                    part = total & (15 << (4 * f))
                else:
                    part = lax.shift_right_logical(total, 28)
                at = pl.multiple_of(f * WORDS + i * 16, 16)
                counts[slot, pl.ds(at, 16), pl.ds(half * 128, 128)] = part.astype(jnp.float32).astype(jnp.bfloat16)
            return carry

        lax.fori_loop(0, WORDS // 16, block, 0, unroll=4)


def multiply(counts, everything, total, slots, rows=slice(None)):
    part = total[rows, :]
    for slot in slots:
        part = part + jnp.dot(counts[slot, rows, :], everything[slot], preferred_element_type=jnp.float32)
    total[rows, :] = part


def towards(group, first, last, do):
    x, z = group // DEPTH, group % DEPTH
    span = last - first

    def step(i, carry):
        there = first + lax.rem(z + i, span)
        for dx in (2, 1, 3, 0):
            device = lax.rem(x + dx, WIDTH) * DEPTH + there

            @pl.when(device != group)
            def _():
                do(device)

        return carry

    lax.fori_loop(0, span, step, 0)


def greet(barrier, group, row, near, early):
    def signal(group_there, row_there):
        pl.semaphore_signal(barrier, inc=1, device_id=(group_there, row_there), device_id_type=MESH)

    @pl.when(early)
    def _():
        towards(group, EARLY, DEPTH, lambda device: signal(device, row))
        towards(group, 0, EARLY, lambda device: signal(device, row))

    for peer in near:
        signal(group, peer)


def swap(group, row, early, outgoing, incoming, swap_send, swap_recv, late_sem, all_sem, meanwhile):
    x, z = group // DEPTH, group % DEPTH

    def send(target):
        pltpu.make_async_remote_copy(
            src_ref=outgoing.at[target], dst_ref=incoming.at[group], send_sem=swap_send, recv_sem=swap_recv,
            device_id=(target, row), device_id_type=MESH,
        ).start()

    def tell(semaphore, target):
        pl.semaphore_signal(semaphore, inc=1, device_id=(target, row), device_id_type=MESH)

    towards(group, 0, EARLY, send)

    @pl.when(jnp.logical_not(early))
    def _():
        towards(group, 0, EARLY, lambda target: tell(late_sem, target))

    meanwhile()

    @pl.when(early)
    def _():
        pl.semaphore_wait(late_sem, WIDTH * (DEPTH - EARLY))
        for partner in range(EARLY, DEPTH, EARLY):

            @pl.when(z + partner < DEPTH)
            def _():
                tell(all_sem, x * DEPTH + z + partner)

    @pl.when(jnp.logical_not(early))
    def _():
        pl.semaphore_wait(all_sem, 1)

    towards(group, EARLY, DEPTH, send)


def exchange_kernel(
    grads_hbm, ids_hbm, lens_hbm, sums_hbm, gathered_hbm, spill_hbm,
    grads, ids, lens, outgoing, incoming, everything, keys, words, adds, counts, total, spill,
    load_sem, sum_sem, out_sem, swap_send, swap_recv, late_sem, all_sem, ring_send, ring_recv,
):
    group = lax.axis_index("group")
    row = lax.axis_index("row")
    z = group % DEPTH
    y, core = row // 2, row % 2

    def at(step, other):
        return lax.rem(y + step + RINGS, RINGS) * 2 + (1 - core if other else core)

    loads = [
        pltpu.make_async_copy(grads_hbm, grads, load_sem.at[0]),
        pltpu.make_async_copy(ids_hbm, ids, load_sem.at[1]),
        pltpu.make_async_copy(lens_hbm, lens, load_sem.at[2]),
    ]
    for load in loads:
        load.start()

    barrier = pltpu.get_barrier_semaphore()
    near = [at(2, False), at(-2, False), at(1, False), at(-1, False), at(0, True)]
    early = z < EARLY
    greet(barrier, group, row, near, early)
    loads[0].wait()
    outgoing[...] = jnp.swapaxes(grads[...].astype(jnp.float32), 0, 1).astype(jnp.bfloat16)
    incoming[group] = outgoing[group]

    def count_all():
        loads[1].wait()
        loads[2].wait()
        prepare(ids, lens, keys, row * TOUCHED)
        compact(keys, words, adds, spill)

        def one(slot, carry):
            count(words, adds, counts, slot)
            return carry

        lax.fori_loop(0, SHARDS, one, 0)
        total[...] = jnp.zeros((TOUCHED, E), jnp.float32)

    pl.semaphore_wait(barrier, jnp.where(early, WIDTH * EARLY - 1, WIDTH * EARLY) + len(near))
    swap(group, row, early, outgoing, incoming, swap_send, swap_recv, late_sem, all_sem, count_all)

    swapped = pltpu.make_async_copy(incoming.at[pl.ds(0, GROUPS - 1)], incoming.at[pl.ds(0, GROUPS - 1)], swap_recv)
    swapped.wait()
    everything[row] = incoming[...].astype(jnp.float32).reshape(CHUNK, E).astype(jnp.bfloat16)

    sent = []
    kept = []

    def pass_on(slot, peer):
        copy = pltpu.make_async_remote_copy(
            src_ref=everything.at[slot], dst_ref=everything.at[slot], send_sem=ring_send.at[len(sent)],
            recv_sem=ring_recv.at[slot], device_id=(group, peer), device_id_type=MESH,
        )
        copy.start()
        sent.append(copy)

    def keep(slot):
        copy = pltpu.make_async_copy(everything.at[slot], gathered_hbm.at[slot], out_sem.at[len(kept)])
        copy.start()
        kept.append(copy)

    def arrive(slot):
        pltpu.make_async_copy(everything.at[slot], everything.at[slot], ring_recv.at[slot]).wait()

    mine = [at(s, False) for s in range(RINGS)]
    theirs = [at(s, True) for s in range(RINGS)]
    for peer in near:
        pass_on(row, peer)
    keep(row)
    arrive(theirs[0])
    keep(theirs[0])
    multiply(counts, everything, total, [row, theirs[0]])
    for s in (-2, 2):
        arrive(mine[s])
    way = 1 - 2 * core
    pass_on(at(-2 * way, False), at(2 * way, False))
    pass_on(mine[-2], mine[1])
    pass_on(mine[2], mine[-1])
    pass_on(mine[-2], theirs[0])
    pass_on(mine[2], theirs[0])
    for s in (-1, 1):
        arrive(mine[s])
        pass_on(mine[s], theirs[0])
    multiply(counts, everything, total, [mine[s] for s in (-2, 2, -1, 1)])
    for s in (-2, 2, -1, 1):
        arrive(theirs[s])
    multiply(counts, everything, total, [theirs[s] for s in (-2, 2, -1, 1)])
    for s in (-2, 2, -1, 1):
        keep(mine[s])
        keep(theirs[s])
    for s in (-3, 3, 4):
        arrive(mine[s])
        pass_on(mine[s], theirs[0])
    multiply(counts, everything, total, [mine[s] for s in (-3, 3, 4)])
    for s in (-3, 3, 4):
        keep(mine[s])
    for s in (-3, 3, 4):
        arrive(theirs[s])
        keep(theirs[s])
    written = [pltpu.make_async_copy(spill, spill_hbm, load_sem.at[3])]
    written[0].start()
    for i in range(BLOCKS):
        at_rows = pl.ds(i * BLOCK, BLOCK)
        multiply(counts, everything, total, [theirs[s] for s in (-3, 3, 4)], at_rows)
        written.append(pltpu.make_async_copy(total.at[at_rows], sums_hbm.at[at_rows], sum_sem.at[i]))
        written[-1].start()
    pltpu.make_async_copy(outgoing.at[pl.ds(0, GROUPS - 1)], outgoing.at[pl.ds(0, GROUPS - 1)], swap_send).wait()
    for copy in sent:
        copy.wait_send()
    for copy in kept + written:
        copy.wait()


def update_kernel(
    sums_hbm, spill_hbm, rows_hbm, state_hbm, ids_hbm, lens_hbm, gathered_hbm, new_rows_hbm, new_state_hbm,
    sums, spill, rows, state, new_rows, new_state, ids, lens, grads, sum_sem, row_sem, out_sem, sem,
):
    parts = [pl.ds(i * PART, PART) for i in range(PARTS)]
    spill_load = pltpu.make_async_copy(spill_hbm, spill, sem.at[0])
    state_load = pltpu.make_async_copy(state_hbm, state, sem.at[1])
    sum_loads = [pltpu.make_async_copy(sums_hbm.at[at], sums.at[at], sum_sem.at[i]) for i, at in enumerate(parts)]
    row_loads = [pltpu.make_async_copy(rows_hbm.at[at], rows.at[at], row_sem.at[i]) for i, at in enumerate(parts)]
    state_load.start()
    for sum_load, row_load in zip(sum_loads, row_loads):
        sum_load.start()
        row_load.start()
    spill_load.start()

    def finish(first):
        outs = []
        for i, at_part in enumerate(parts):
            if first:
                sum_loads[i].wait()
                row_loads[i].wait()
            for j in range(i * PART // 128, (i + 1) * PART // 128):
                at = pl.ds(j * 128, 128)
                part = sums[at, :]
                if first:
                    field = j * 128 // WORDS
                    part = part * (2.0 ** (-4 * field) if field < FIELDS - 1 else 1.0)
                fresh = state[:, at] + jnp.sum((part * part).T, axis=0, keepdims=True) * (1.0 / E)
                new_state[:, at] = fresh
                scale = 0.5 / (jnp.sqrt(fresh) + 1e-08)
                new_rows[at, :] = rows[at, :] - part * jnp.broadcast_to(scale, (128, 128)).T
            outs.append(pltpu.make_async_copy(new_rows.at[at_part], new_rows_hbm.at[at_part], out_sem.at[i]))
            outs[-1].start()
        outs.append(pltpu.make_async_copy(new_state, new_state_hbm, out_sem.at[PARTS]))
        outs[-1].start()
        return outs

    state_load.wait()
    outs = finish(True)
    spill_load.wait()
    spilled = jnp.max(spill[...]) >= 0
    for out in outs:
        out.wait()

    @pl.when(spilled)
    def _():
        base = lax.axis_index("row") * TOUCHED
        for source, target in ((ids_hbm, ids), (lens_hbm, lens), (gathered_hbm, grads)):
            copy = pltpu.make_async_copy(source, target, sem.at[2])
            copy.start()
            copy.wait()
        exact = sums
        exact[...] = jnp.zeros((TOUCHED, E), jnp.float32)
        column = lax.broadcasted_iota(jnp.int32, (128, 128), 0)

        def samples(t, carry):
            lanes = pl.ds(pl.multiple_of(t * 128, 128), 128)
            part = grads[t // 2, pl.ds(pl.multiple_of((t % 2) * 128, 128), 128), :]
            used = lens[:, lanes]

            def touched(i, carry):
                here = column + (base + i * 128)

                def add(q, found):
                    eight = ids[pl.ds(pl.multiple_of(q * 8, 8), 8), lanes]
                    for s in range(8):
                        hit = (eight[s : s + 1] == here) & (q * 8 + s < used)
                        found = found + jnp.where(hit, 1.0, 0.0)
                    return found

                found = lax.fori_loop(0, SLOTS // 8, add, jnp.zeros((128, 128), jnp.float32))
                at = pl.ds(pl.multiple_of(i * 128, 128), 128)
                exact[at, :] = exact[at, :] + jnp.dot(
                    found.astype(jnp.bfloat16), part, preferred_element_type=jnp.float32
                )
                return carry

            return lax.fori_loop(0, TOUCHED // 128, touched, carry)

        lax.fori_loop(0, SAMPLES // 128, samples, 0)
        for out in finish(False):
            out.wait()


def on_device(pooled_grad, bag_ids, bag_len, table_rows, row_state):
    ids = bag_ids.reshape(SLOTS, SAMPLES)
    rows = table_rows.reshape(TOUCHED, E)
    hbm = pl.BlockSpec(memory_space=pltpu.HBM)
    sums, gathered, spill = pl.pallas_call(
        exchange_kernel,
        out_shape=(
            jax.ShapeDtypeStruct((TOUCHED, E), jnp.float32),
            jax.ShapeDtypeStruct((SHARDS, CHUNK, E), jnp.bfloat16),
            jax.ShapeDtypeStruct((8, 128), jnp.int32),
        ),
        in_specs=[hbm] * 3,
        out_specs=(hbm,) * 3,
        scratch_shapes=[
            pltpu.VMEM((SAMPLES // SHARDS // GROUPS, GROUPS, E), jnp.bfloat16),
            pltpu.VMEM((SLOTS, SAMPLES), jnp.int32),
            pltpu.VMEM((1, SAMPLES), jnp.int32),
            pltpu.VMEM((GROUPS, CHUNK // GROUPS, E), jnp.bfloat16),
            pltpu.VMEM((GROUPS, CHUNK // GROUPS, E), jnp.bfloat16),
            pltpu.VMEM((SHARDS, CHUNK, E), jnp.bfloat16),
            pltpu.VMEM((SLOTS // 8, SAMPLES // 16, 128), jnp.int32),
            pltpu.VMEM((KEPT, SAMPLES // 128, 128), jnp.int32),
            pltpu.VMEM((KEPT, SAMPLES // 128, 128), jnp.int32),
            pltpu.VMEM((SHARDS, TOUCHED, CHUNK), jnp.bfloat16),
            pltpu.VMEM((TOUCHED, E), jnp.float32),
            pltpu.VMEM((8, 128), jnp.int32),
            pltpu.SemaphoreType.DMA((4,)),
            pltpu.SemaphoreType.DMA((BLOCKS,)),
            pltpu.SemaphoreType.DMA((SHARDS,)),
            pltpu.SemaphoreType.DMA,
            pltpu.SemaphoreType.DMA,
            pltpu.SemaphoreType.REGULAR,
            pltpu.SemaphoreType.REGULAR,
            pltpu.SemaphoreType.DMA((16,)),
            pltpu.SemaphoreType.DMA((SHARDS,)),
        ],
        compiler_params=pltpu.CompilerParams(collective_id=0, has_side_effects=True, vmem_limit_bytes=VMEM),
        name="exchange_and_count",
    )(pooled_grad, ids, bag_len)
    new_rows, new_state = pl.pallas_call(
        update_kernel,
        out_shape=(
            jax.ShapeDtypeStruct((TOUCHED, E), jnp.float32),
            jax.ShapeDtypeStruct((1, TOUCHED), jnp.float32),
        ),
        in_specs=[hbm] * 7,
        out_specs=(hbm, hbm),
        scratch_shapes=[
            pltpu.VMEM((TOUCHED, E), jnp.float32),
            pltpu.VMEM((8, 128), jnp.int32),
            pltpu.VMEM((TOUCHED, E), jnp.float32),
            pltpu.VMEM((1, TOUCHED), jnp.float32),
            pltpu.VMEM((TOUCHED, E), jnp.float32),
            pltpu.VMEM((1, TOUCHED), jnp.float32),
            pltpu.VMEM((SLOTS, SAMPLES), jnp.int32),
            pltpu.VMEM((1, SAMPLES), jnp.int32),
            pltpu.VMEM((SHARDS, CHUNK, E), jnp.bfloat16),
            pltpu.SemaphoreType.DMA((PARTS,)),
            pltpu.SemaphoreType.DMA((PARTS,)),
            pltpu.SemaphoreType.DMA((PARTS + 1,)),
            pltpu.SemaphoreType.DMA((3,)),
        ],
        compiler_params=pltpu.CompilerParams(vmem_limit_bytes=VMEM),
        name="update",
    )(sums, spill, rows, row_state, ids, bag_len, gathered)
    return (new_rows.reshape(1, TOUCHED, E), new_state)


def solution(mesh):
    placed = (
        P(("row", "group"), None, None),
        P("group", None, None),
        P("group", None),
        P("group", "row", None),
        P("group", "row"),
    )
    return jax.shard_map(
        on_device,
        mesh=mesh,
        in_specs=placed,
        out_specs=(P("group", "row", None), P("group", "row")),
        check_vma=False,
    )
```

time: 354 us -> 50.2 us (0.14)
  the two profiles are of different devices: /device:TPU:1 before, /device:TPU:392 now
where the time goes in v1:
time: 50.2 us; the launch traced here: 50.1 us
  Pallas kernels  49.4 us (98%)
  between operations  0.64 us (1%)
    pallas_call x1, Pallas kernels, on_device(): pl.pallas_call(exchange_kernel, out_shape=(jax.ShapeDtypeStruct((TOUCHED,...  46.3 us
    pallas_call x1, Pallas kernels, on_device(): pl.pallas_call(update_kernel, out_shape=(jax.ShapeDtypeStruct((TOUCHED, E...  3.15 us

profile of v1, /device:TPU:392, one launch (start us, length us, event | category | flops | bytes accessed | tf_op | source)
XLA Modules:
  0.0 50.1 jit_solution(1708007044105953192)
XLA Ops:
  0.6 46.3 %exchange_and_count.1 = (f32[2048,128]{1,0:T(8,128)}, bf16[16,256,128]{2,1,0:T(8,128)(2,1)}, s32[8,128]{1,0:T(8,128)}) custom-call(bf16[4,64,128]{2,1,0:T(8,128)(2,1)} %grads_hbm.1, s32[40,4096]{1,0:T(8,128)} %bitcast.3, s32[1,4096]{1,0:T(1,128)} %lens_hbm.3), custom_call_target="tpu_custom_call" | custom-call | tf_op jit(solution)/shard_map/exchange_and_count/pallas_call | solution.py:379
  46.9 3.1 %update.1 = (f32[2048,128]{1,0:T(8,128)}, f32[1,2048]{1,0:T(1,128)}) custom-call(f32[2048,128]{1,0:T(8,128)} %get-tuple-element.7.sums_hbm, s32[8,128]{1,0:T(8,128)} %get-tuple-element.8.spill_hbm, f32[2048,128]{1,0:T(8,128)} %bitcast.5, f32[1,2048]{1,0:T(1,128)} %state_hbm.1, s32[40,4096]{1,0:T(8,128)} %bitcast.4, s32[1,4096]{1,0:T(1,128)} %lens_hbm.3, ...), custom_call_target="tpu_custom_call" | custom-call | tf_op jit(solution)/shard_map/update/pallas_call | solution.py:414

commit v2 on v1

--- a/solution.py
+++ b/solution.py
@@ -15,7 +15,7 @@
 WIDTH = 4
 DEPTH = 16
 RINGS = 8
-EARLY = 6
+EARLY = 7
 VMEM = 60 * 2**20
 TOUCHED = 2048
 BLOCKS = 4
@@ -158,11 +158,12 @@
     @pl.when(early)
     def _():
         pl.semaphore_wait(late_sem, WIDTH * (DEPTH - EARLY))
-        for partner in range(EARLY, DEPTH, EARLY):
-
-            @pl.when(z + partner < DEPTH)
-            def _():
-                tell(all_sem, x * DEPTH + z + partner)
+        for there in range(EARLY, DEPTH):
+            source = EARLY - 1 if there - (EARLY - 1) <= DEPTH - there else 0
+
+            @pl.when(z == source)
+            def _(there=there):
+                tell(all_sem, x * DEPTH + there)
 
     @pl.when(jnp.logical_not(early))
     def _():

time: 50.2 us -> 49.9 us (level)
  the two profiles are of different devices: /device:TPU:392 before, /device:TPU:1 now
where the time goes in v2:
time: 49.9 us; the launch traced here: 49.7 us
  Pallas kernels  49.1 us (98%)
  between operations  0.64 us (1%)
    pallas_call x1, Pallas kernels, on_device(): pl.pallas_call(exchange_kernel, out_shape=(jax.ShapeDtypeStruct((TOUCHED,...  45.9 us
    pallas_call x1, Pallas kernels, on_device(): pl.pallas_call(update_kernel, out_shape=(jax.ShapeDtypeStruct((TOUCHED, E...  3.15 us

profile of v2, /device:TPU:1, one launch (start us, length us, event | category | flops | bytes accessed | tf_op | source)
XLA Modules:
  0.0 49.7 jit_solution(5067514893510751833)
XLA Ops:
  0.6 45.9 %exchange_and_count.1 = (f32[2048,128]{1,0:T(8,128)}, bf16[16,256,128]{2,1,0:T(8,128)(2,1)}, s32[8,128]{1,0:T(8,128)}) custom-call(bf16[4,64,128]{2,1,0:T(8,128)(2,1)} %grads_hbm.1, s32[40,4096]{1,0:T(8,128)} %bitcast.3, s32[1,4096]{1,0:T(1,128)} %lens_hbm.3), custom_call_target="tpu_custom_call" | custom-call | tf_op jit(solution)/shard_map/exchange_and_count/pallas_call | solution.py:380
  46.6 3.1 %update.1 = (f32[2048,128]{1,0:T(8,128)}, f32[1,2048]{1,0:T(1,128)}) custom-call(f32[2048,128]{1,0:T(8,128)} %get-tuple-element.7.sums_hbm, s32[8,128]{1,0:T(8,128)} %get-tuple-element.8.spill_hbm, f32[2048,128]{1,0:T(8,128)} %bitcast.5, f32[1,2048]{1,0:T(1,128)} %state_hbm.1, s32[40,4096]{1,0:T(8,128)} %bitcast.4, s32[1,4096]{1,0:T(1,128)} %lens_hbm.3, ...), custom_call_target="tpu_custom_call" | custom-call | tf_op jit(solution)/shard_map/update/pallas_call | solution.py:415
